TPU v7x, 512 devices: a whole 4x8x8 slice. The times are simulated.
512 devices in a mesh: dp: 16 (over y, z_lo), tensor: 32 (over z_hi, x, core).
Axes of the slice: x: 4, y: 8, z: 8 (z_hi: 4, z_lo: 2; z = z_hi * 2 + z_lo), core: 2. Of those that a mesh axis runs over, the one named last changes fastest.
Arguments:
- tokens: bfloat16 [512, 8192], P('dp'), may hold values from -6 to 6
- gate_weight: bfloat16 [8192, 16384], P('dp', 'tensor'), may hold values from -0.0625 to 0.0625
- up_weight: bfloat16 [8192, 16384], P('dp', 'tensor'), may hold values from -0.0625 to 0.0625
- down_weight: bfloat16 [16384, 8192], P('tensor', 'dp'), may hold values from -6 to 6
- pruned_blocks: int32 [2], replicated, may hold values from 0 to 127, as said below
- panel_number: int32 [1], replicated, may hold values from 0 to 30
Outputs:
- factored_gram: float32 [16384, 16384], P('dp', 'tensor')
- compensation: float32 [16384, 8192], P('tensor', 'dp')
Inputs may be any that keep to these rules, and one draw needn't show every extreme that they name: `pruned_blocks`: 2 distinct block numbers in any order, the last block of hidden units always among them; block b holds hidden units b * 128 to b * 128 + 127. `panel_number`: the panel holds hidden units 512 * p to 512 * p + 511 and some units follow it.
All inputs are finite; a program needn't handle non-finite values.
Results may differ from a plain program's by a relative error of at most 0.012.
The roundings to bfloat16 on the way count: a program that leaves them out, or rounds other values in their place, can miss the bound.
Values may be sent and summed in bfloat16 or wider, within the bound.
A program may use at most 64 MiB of HBM per device.

v0:
```python
import jax
import jax.numpy as jnp
from jax import lax
from jax.sharding import PartitionSpec as P

PANEL = 512
BLOCK = 128
NPRUNE = 2


DAMPING = 0.05
HIGHEST = lax.Precision.HIGHEST


def spread_2(block, axis, owner):
    block = jnp.where(lax.axis_index(axis) == owner, block, jnp.zeros_like(block))
    return lax.psum(block, axis)


def lower_solve(lower_factor, right_side):
    return lax.linalg.triangular_solve(lower_factor, right_side, left_side=True, lower=True)


def right_lower_solve(lower_factor, columns):
    return lax.linalg.triangular_solve(
        lower_factor, columns, left_side=False, lower=True, transpose_a=True
    )


def kept_flags(channel, pruned_blocks):
    return jnp.all((channel // BLOCK)[:, None] != pruned_blocks[None, :], axis=1)


def factor_rows(lower_factor, panel_columns, channel, panel_first):
    solved = right_lower_solve(lower_factor, panel_columns)
    return jnp.where((channel >= panel_first + PANEL)[:, None], solved, 0.0)


def tokens_product(left_side, right_side):
    return lax.dot_general(
        left_side, right_side, (((0,), (0,)), ((), ())), preferred_element_type=jnp.float32
    )


def kept_block(left_side, right_side, left_channel, right_channel, pruned_blocks, total_tokens):
    raw_gram = tokens_product(left_side, right_side) / total_tokens
    left_kept = kept_flags(left_channel, pruned_blocks)
    right_kept = kept_flags(right_channel, pruned_blocks)
    masked = jnp.where(left_kept[:, None] & right_kept[None, :], raw_gram, 0.0)
    diagonal = jnp.where(left_kept, DAMPING, 1.0)
    return masked + jnp.where(
        left_channel[:, None] == right_channel[None, :], diagonal[:, None], 0.0
    )


def local(tokens, gate_weight, up_weight, down_weight, pruned_blocks, panel_number):
    row_groups = lax.axis_size("dp")
    column_groups = lax.axis_size("tensor")
    row_index = lax.axis_index("dp")
    column_index = lax.axis_index("tensor")
    local_tokens = tokens.shape[0]
    total_tokens = local_tokens * row_groups
    column_width = gate_weight.shape[1]
    full_width = column_width * column_groups
    row_width = full_width // row_groups
    spread = column_groups // row_groups
    features = lax.all_to_all(tokens, "dp", split_axis=1, concat_axis=0, tiled=True)
    weights = jnp.concatenate([gate_weight, up_weight], axis=1)
    partial_value = jnp.dot(features, weights, preferred_element_type=jnp.float32)
    summed = lax.psum(partial_value, "dp")
    hidden_cols = (jax.nn.silu(summed[:, :column_width]) * summed[:, column_width:]).astype(
        jnp.bfloat16
    )
    pieces = []
    for offset in range(spread):
        pieces.append(spread_2(hidden_cols, "tensor", row_index * spread + offset))
    row_hidden = jnp.concatenate(pieces, axis=1)
    row_channel = row_index * row_width + lax.iota(jnp.int32, row_width)
    column_channel = column_index * column_width + lax.iota(jnp.int32, column_width)
    kept_gram = kept_block(
        row_hidden, hidden_cols, row_channel, column_channel, pruned_blocks, total_tokens
    )
    hidden_parts = []
    down_parts = []
    for number in range(NPRUNE):
        first_channel = pruned_blocks[number] * BLOCK
        local_first = jnp.clip(first_channel - column_index * column_width, 0, column_width - BLOCK)
        hidden_piece = lax.dynamic_slice_in_dim(hidden_cols, local_first, BLOCK, 1)
        down_piece = lax.dynamic_slice_in_dim(down_weight, local_first, BLOCK, 0)
        got_hidden, got_down = (
            spread_2(hidden_piece, "tensor", first_channel // column_width),
            spread_2(down_piece, "tensor", first_channel // column_width),
        )
        hidden_parts.append(got_hidden)
        down_parts.append(got_down)
    pruned_hidden = jnp.concatenate(hidden_parts, axis=1)
    pruned_down = jnp.concatenate(down_parts, axis=0)
    column_kept = kept_flags(column_channel, pruned_blocks)
    cross_values = tokens_product(hidden_cols, pruned_hidden) / total_tokens
    cross_gram = jnp.where(column_kept[:, None], cross_values, 0.0).astype(jnp.bfloat16)
    right_block = jnp.dot(cross_gram, pruned_down, preferred_element_type=jnp.float32)
    panel_first = panel_number[0] * PANEL
    panel_channel = panel_first + lax.iota(jnp.int32, PANEL)
    column_offset = jnp.clip(panel_first - column_index * column_width, 0, column_width - PANEL)
    row_offset = jnp.clip(panel_first - row_index * row_width, 0, row_width - PANEL)
    column_owner = panel_first // column_width
    panel_hidden = spread_2(hidden_cols, "tensor", column_owner)
    row_panel = kept_block(
        row_hidden, panel_hidden, row_channel, panel_channel, pruned_blocks, total_tokens
    )
    diag_panel = kept_block(
        panel_hidden, panel_hidden, panel_channel, panel_channel, pruned_blocks, total_tokens
    )
    lower_factor = jnp.linalg.cholesky(diag_panel)
    row_factor = factor_rows(lower_factor, row_panel, row_channel, panel_first)
    column_panel = kept_block(
        hidden_cols, panel_hidden, column_channel, panel_channel, pruned_blocks, total_tokens
    )
    column_factor = factor_rows(lower_factor, column_panel, column_channel, panel_first)
    panel_kept = kept_flags(panel_channel, pruned_blocks)
    panel_values = tokens_product(panel_hidden, pruned_hidden) / total_tokens
    panel_cross = jnp.where(panel_kept[:, None], panel_values, 0.0).astype(jnp.bfloat16)
    panel_right = jnp.dot(panel_cross, pruned_down, preferred_element_type=jnp.float32)
    factored = kept_gram - jnp.dot(row_factor, column_factor.T, precision=HIGHEST)
    row_below = row_channel >= panel_first + PANEL
    row_in_panel = (row_channel >= panel_first) & (row_channel < panel_first + PANEL)
    column_in_panel = (column_channel >= panel_first) & (column_channel < panel_first + PANEL)
    zeros_block = jnp.zeros_like(factored)
    factored = jnp.where(row_below[:, None] & column_in_panel[None, :], row_factor, factored)
    placed_lower = lax.dynamic_update_slice(zeros_block, lower_factor, (row_offset, column_offset))
    factored = jnp.where(row_in_panel[:, None] & column_in_panel[None, :], placed_lower, factored)
    solved = lower_solve(lower_factor, panel_right)
    compensation = right_block - jnp.dot(column_factor, solved, precision=HIGHEST)
    compensation = jnp.where(column_in_panel[:, None], solved, compensation)
    return (factored, compensation)


def solution(mesh):
    in_specs = (P("dp", None), P("dp", "tensor"), P("dp", "tensor"), P("tensor", "dp"), P(), P())
    out_specs = (P("dp", "tensor"), P("tensor", "dp"))
    return jax.shard_map(local, mesh=mesh, in_specs=in_specs, out_specs=out_specs, check_vma=False)
```

profile of v0, /device:TPU:16, one launch (start us, length us, event | category | flops | bytes accessed | tf_op | source)
XLA Modules:
  0.0 715.8 jit_solution(15812953370170320570)
XLA Ops:
  8.4 24.3 %all_to_all.19 = bf16[32,16,512]{2,0,1:T(8,128)(2,1)S(1)} all-to-all(bf16[32,16,512]{2,0,1:T(8,128)(2,1)S(1)} %bitcast.90), channel_id=1, replica_groups=mesh['dp'=16,'tensor'=32] {'dp'}, dimensions={1} | all-to-all | bytes 1048576 | tf_op jit(solution)/shard_map/all_to_all | solution.py:67
  32.7 2.1 convolution_bitcast_fusion
  38.4 147.6 %all-reduce.5.cloned.1.call-done = f32[512,1024]{0,1:T(8,128)} async-done(((f32[512,1024]{0,1:T(8,128)}), f32[512,1024]{0,1:T(8,128)}) %all-reduce.5.cloned.1.call-update) | async-done | bytes 2097168 | tf_op jit(solution)/shard_map/psum | solution.py:70
  186.0 2.7 broadcast_select_fusion
  195.0 295.6 %all-reduce.7.cloned.1.call-done = (bf16[512,512]{0,1:T(8,128)(2,1)}, bf16[512,512]{0,1:T(8,128)(2,1)}, bf16[512,512]{0,1:T(8,128)(2,1)}, bf16[128,512]{1,0:T(8,...) async-done(((bf16[512,512]{0,1:T(8,128)(2,1)}, bf16[512,512]{0,1:T(8,128)(2,1)}, bf16[512,512]{0,1:T(8,128)(2,1)}, ...) | async-done | bytes 2097168 | tf_op jit(solution)/shard_map/psum | solution.py:17
  493.6 2.5 and_select_fusion
  500.5 11.7 %cholesky.103 = f32[128,128]{1,0:T(8,128)S(1)} custom-call(f32[128,128]{1,0:T(8,128)S(1)} %cholesky.263), custom_call_target="Cholesky" | custom-call | tf_op jit(solution)/shard_map/jit(cholesky)/cholesky | solution.py:114
  512.4 9.8 %custom-call.34 = f32[1,128,128]{1,2,0:T(8,128)S(1)} custom-call(f32[1,128,128]{2,1,0:T(8,128)S(1)} %get-tuple-element.48), custom_call_target="InvertDiagBlocksLowerTriangular" | custom-call | tf_op jit(solution)/shard_map/jit(cholesky)/cholesky | solution.py:114
  522.9 12.0 %cholesky.215 = f32[128,128]{1,0:T(8,128)S(1)} custom-call(f32[128,128]{1,0:T(8,128)S(1)} %cholesky.267), custom_call_target="Cholesky" | custom-call | tf_op jit(solution)/shard_map/jit(cholesky)/cholesky | solution.py:114
  534.9 9.8 %custom-call.35 = f32[1,128,128]{1,2,0:T(8,128)S(1)} custom-call(f32[1,128,128]{2,1,0:T(8,128)S(1)} %get-tuple-element.45), custom_call_target="InvertDiagBlocksLowerTriangular" | custom-call | tf_op jit(solution)/shard_map/jit(cholesky)/cholesky | solution.py:114
  545.4 11.7 %cholesky.236 = f32[128,128]{1,0:T(8,128)S(1)} custom-call(f32[128,128]{1,0:T(8,128)S(1)} %cholesky.272), custom_call_target="Cholesky" | custom-call | tf_op jit(solution)/shard_map/jit(cholesky)/cholesky | solution.py:114
  557.1 9.8 %custom-call.36 = f32[1,128,128]{1,2,0:T(8,128)S(1)} custom-call(f32[1,128,128]{2,1,0:T(8,128)S(1)} %get-tuple-element.42), custom_call_target="InvertDiagBlocksLowerTriangular" | custom-call | tf_op jit(solution)/shard_map/jit(cholesky)/cholesky | solution.py:114
  567.5 24.7 %cholesky.253 = f32[128,128]{1,0:T(8,128)S(1)} custom-call(f32[128,128]{1,0:T(8,128)S(1)} %convolution_subtract_fusion.11), custom_call_target="Cholesky" | custom-call | tf_op jit(solution)/shard_map/jit(cholesky)/cholesky | solution.py:114
  593.6 1.9 constant_dynamic-update-slice_fusion.1
  599.9 10.5 %while.1 = (s32[]{:T(128)}, f32[512,512]{1,0:T(8,128)S(1)}, s32[4,2]{0,1:T(2,128)S(1)}, f32[4,128,128]{2,1,0:T(8,128)}, s32[]{:T(128)}) while((s32[]{:T(128)}, f32[512,512]{1,0:T(8,128)S(1)}, s32[4,2]{0,1:T(2,128)S(1)}, f32[4,128,128]{2,1,0:T(8,128)}, s32[]{:T(128)}) %tuple.42), condition=%wide.while_cond, body=%wide.while_body.sunk | while | flops 2 | bytes 132205 | solution.py:25
  600.6 2.0 bitcast_dynamic-update-slice_fusion.2
  603.2 2.0 bitcast_dynamic-update-slice_fusion.2
  605.8 2.0 bitcast_dynamic-update-slice_fusion.2
  608.5 2.0 bitcast_dynamic-update-slice_fusion.2
  610.5 40.1 %custom-call.37 = f32[4,128,128]{1,2,0:T(8,128)S(1)} custom-call(f32[4,128,128]{2,1,0:T(8,128)} %get-tuple-element.9), custom_call_target="InvertDiagBlocksLowerTriangular" | custom-call | tf_op jit(solution)/shard_map/triangular_solve | solution.py:25
  650.6 1.9 constant_dynamic-update-slice_fusion
  652.5 2.3 select_add_fusion
  657.0 1.8 convolution_subtract_fusion.1
  660.3 3.5 fusion.9
  663.7 2.0 copy.88
  672.3 2.2 convolution_subtract_fusion.8
  683.0 2.4 fusion.94
  685.4 2.0 fusion.93
  692.9 4.1 dynamic_update_slice.4
  697.1 4.4 fusion.6
  701.6 3.6 fusion.18
  705.3 3.3 select_select_fusion
  (156 shorter events, 48.3 us)
Async XLA Ops:
  7.2 25.6 %copy-start.9 = (bf16[512,512]{1,0:T(8,128)(2,1)S(1)}, bf16[512,512]{1,0:T(8,128)(2,1)}, u32[]{:S(2)}) copy-start(bf16[512,512]{1,0:T(8,128)(2,1)} %param.8) | copy-start | bytes 1572868
  7.2 25.6 %copy-start.10 = (bf16[512,512]{1,0:T(8,128)(2,1)S(1)}, bf16[512,512]{1,0:T(8,128)(2,1)}, u32[]{:S(2)}) copy-start(bf16[512,512]{1,0:T(8,128)(2,1)} %param.7) | copy-start | bytes 1572868
  7.2 178.8 %all-reduce.5.cloned.1.call-start = ((), (), s32[]{:S(2)}) async-start(), calls=%async_computation.1 | async-start | bytes 4194304 | tf_op jit(solution)/shard_map/psum | solution.py:70
  32.7 2.8 copy-start.24
  32.7 4.9 copy-start.20
  34.8 455.8 %all-reduce.7.cloned.1.call-start = ((), (), s32[]{:S(2)}) async-start(), calls=%async_computation.2 | async-start | bytes 4194304 | tf_op jit(solution)/shard_map/psum | solution.py:17
  194.9 457.6 %copy-start.25 = (s32[1024]{0:T(1024)}, s32[1024]{0:T(1024)S(1)}, u32[]{:S(2)}) copy-start(s32[1024]{0:T(1024)S(1)} %iota_add_fusion) | copy-start | bytes 12292
  195.0 457.5 %copy-start.27 = (pred[1024]{0:T(1024)(128)(4,1)}, pred[1024]{0:T(1024)(128)(4,1)S(1)}, u32[]{:S(2)}) copy-start(pred[1024]{0:T(1024)(128)(4,1)S(1)} %compare_reduce_fusion) | copy-start | bytes 3076
  598.7 53.8 %copy-start = (bf16[512,512]{0,1:T(8,128)(2,1)S(1)}, bf16[512,512]{0,1:T(8,128)(2,1)}, u32[]{:S(2)}) copy-start(bf16[512,512]{0,1:T(8,128)(2,1)} %get-tuple-element.20) | copy-start | bytes 1572868
  671.8 6.4 copy-start.21
  672.3 5.9 copy-start.23
  672.3 5.9 copy-start.22
  689.5 1.8 copy-start.7
  690.1 2.8 copy-start.2
  691.3 5.7 copy-start.6
  691.3 5.7 copy-start.8
  691.3 5.7 copy-start.31
  691.3 5.7 copy-start.32
  697.0 4.5 copy-start.11
  697.0 4.4 copy-start.12
  697.0 4.4 copy-start.13
  697.1 4.4 copy-start.14
  697.1 4.4 copy-start.16
  697.1 4.4 copy-start.17
  697.1 4.4 copy-start.18
  697.1 4.4 copy-start.19
  697.1 4.4 copy-start.29
  701.5 3.7 copy-start.3
  701.6 3.7 copy-start.15
  701.6 3.7 copy-start.26
  701.6 3.7 copy-start.28
  701.6 3.7 copy-start.30
  (3 other events, 2.2 us)
Sparse Core Ops, SparseCore 0:
  35.0 150.9 all-reduce.4
  190.6 299.9 all-reduce.6
where the time goes:
time: 726 us; the launch traced here: 716 us
  waiting for transfers between devices  443 us (61%)
  other arithmetic  144 us (20%)
  matrix products  45.6 us (6%)
  local copies, waits for them, and re-layouts  38.5 us (5%)
  blocking collectives  24.3 us (3%)
  between operations  19.8 us (3%)
    psum x1, waiting for transfers between devices, spread_2(): return lax.psum(block, axis)  296 us
    psum x1, waiting for transfers between devices, local(): summed = lax.psum(partial_value, 'dp')  148 us
    another operation x14, other arithmetic, local(): lower_factor = jnp.linalg.cholesky(diag_panel)  91.7 us
    another operation x3, other arithmetic, right_lower_solve(): lax.linalg.triangular_solve(lower_factor, columns, left_side=False, lower...  41.4 us
    all_to_all x1, blocking collectives, local(): lax.all_to_all(tokens, 'dp', split_axis=1, concat_axis=0, tiled=True)  24.3 us
    another operation x14, matrix products, right_lower_solve(): lax.linalg.triangular_solve(lower_factor, columns, left_side=False, lower...  17.5 us
  transfers between devices with their start and end apart: 2, of which 2 were waited for; matrix products, arithmetic and copies ran while one was open for 1% of the time, Pallas kernels for 0%

commit v1 on v0

v1 whole, which is shorter than its diff:
```python
import jax
import jax.numpy as jnp
from jax import lax
from jax.experimental import pallas as pl
from jax.experimental.pallas import tpu as pltpu
from jax.sharding import PartitionSpec as P

F32 = jnp.float32
BF16 = jnp.bfloat16
MESH = pl.DeviceIdType.MESH
DAMPING = 0.05
NDP = 16
NT = 32
NY = 8
WIDTH = 4

CHAINS = ((1, 0, 4), (-1, 1, 4), (1, 1, 3), (-1, 0, 3))


def split(x):
    hi = x.astype(BF16)
    return hi, (x - hi.astype(F32)).astype(BF16)


def dot(a, b, ca=1, cb=0):
    return lax.dot_general(a, b, (((ca,), (cb,)), ((), ())), preferred_element_type=F32)


def dot3(a, b, ca=1, cb=0):
    ah, al = split(a)
    bh, bl = split(b)
    return dot(ah, bh, ca, cb) + (dot(ah, bl, ca, cb) + dot(al, bh, ca, cb))


def drain(ref, sem):
    pltpu.make_async_copy(ref, ref, sem).wait()


def spread_kernel(
    tok, gate, up, down, pruned, panel,
    rowb, colb, pcb, pd,
    feat, pf, sb, rb, ssum, zr, hch, hpc, hold, obuf, gbuf, dbuf, dhold, dsel,
    s_tok, r_tok, s_sib, r_sib, s_ch, r_ch, s_z, r_z, s_d1, r_d1, s_d2, r_d2,
    s_p, r_p, s_pz, r_pz, s_ps, r_ps, s_row, r_row, s_col, r_col, s_e1, r_e1, s_e2, r_e2,
):
    i = lax.axis_index("dp")
    j = lax.axis_index("tensor")
    y, z = i // 2, i % 2
    zh, x, c = j // 8, (j // 2) % 4, j % 2
    sib = j + 1 - 2 * c
    other_z = i + 1 - 2 * z

    def remote(src, dst, send, recv, to):
        copy = pltpu.make_async_remote_copy(
            src_ref=src, dst_ref=dst, send_sem=send, recv_sem=recv, device_id=to, device_id_type=MESH
        )
        copy.start()
        return copy

    def here(src, dst, sem):
        pltpu.make_async_copy(src, dst, sem).start()

    def unless_self(same, src, dst, send, recv, to):
        @pl.when(same)
        def _():
            here(src, dst, recv)

        @pl.when(jnp.logical_not(same))
        def _():
            remote(src, dst, send, recv, to)

    barrier = pltpu.get_barrier_semaphore()

    def greet_dp(d, _):
        pl.semaphore_signal(barrier, inc=1, device_id=((i + d) % NDP, j), device_id_type=MESH)
        return 0

    def greet_t(d, _):
        pl.semaphore_signal(barrier, inc=1, device_id=(i, (j + d) % NT), device_id_type=MESH)
        return 0

    lax.fori_loop(1, NDP, greet_dp, 0)
    lax.fori_loop(1, NT, greet_t, 0)
    pl.semaphore_wait(barrier, NDP + NT - 2)

    def part(o):
        return tok.at[:, pl.ds(pl.multiple_of(512 * o + 256 * c, 256), 256)]

    mine = pl.ds(pl.multiple_of(32 * i, 32), 32)

    def send_tok(d, _):
        o = (i + d) % NDP
        remote(part(o), feat.at[c, mine, :], s_tok, r_tok, (o, j))
        return 0

    lax.fori_loop(1, NDP, send_tok, 0)
    here(part(i), feat.at[c, mine, :], r_tok)

    for n in range(2):
        quarter = pruned[n] % 4
        for e in range(8):
            rows = [down[128 * k + 16 * e : 128 * k + 16 * e + 16, :] for k in range(4)]
            low = jnp.where(quarter == 0, rows[0], rows[1])
            high = jnp.where(quarter == 2, rows[2], rows[3])
            dbuf[8 * n + e] = jnp.where(quarter < 2, low, high)

    def send_e1(e, _):
        to = 2 * e + e % 2
        unless_self(to == j, dbuf.at[e], dhold.at[j], s_e1, r_e1, (i, to))
        return 0

    lax.fori_loop(0, 16, send_e1, 0)
    is_down_holder = (j // 2) % 2 == c

    drain(feat.at[c], r_tok)
    remote(feat.at[c], feat.at[c], s_sib, r_sib, (i, sib))

    own = pl.ds(pl.multiple_of(256 * c, 256), 256)
    theirs = pl.ds(pl.multiple_of(256 * (1 - c), 256), 256)
    pf[:, :512] = dot(feat[c], gate[own, :])
    pf[:, 512:] = dot(feat[c], up[own, :])
    drain(feat.at[1 - c], r_sib)
    pf[:, :512] += dot(feat[1 - c], gate[theirs, :])
    pf[:, 512:] += dot(feat[1 - c], up[theirs, :])

    def value(yd, h):
        return pf[pl.ds(pl.multiple_of(64 * yd, 64), 64), 512 * h : 512 * h + 512]

    for s in range(1, 5):
        for n, (way, h, hops) in enumerate(CHAINS):
            if s > hops:
                continue
            v = value((y + way * (hops - s + 1) + NY) % NY, h)
            if s > 1:
                drain(rb.at[n, s - 2], r_ch.at[n, s - 2])
                v = v + rb[n, s - 2].astype(F32)
            sb[n, s - 1] = v.astype(BF16)
            to = 2 * ((y + way + NY) % NY) + z
            remote(sb.at[n, s - 1], rb.at[n, s - 1], s_ch.at[n, s - 1], r_ch.at[n, s - 1], (to, j))

    @pl.when(is_down_holder)
    def _():
        e = j // 2
        drain(dhold, r_e1)
        dsel[...] = jnp.where(e < 8, dhold[pruned[0] // 4], dhold[pruned[1] // 4])

        def send_e2(d, _):
            remote(dsel, pd.at[e], s_e2, r_e2, (i, (j + d) % NT))
            return 0

        lax.fori_loop(1, NT, send_e2, 0)
        here(dsel, pd.at[e], r_e2)

    for h in range(2):
        total = value(y, h)
        for n, (way, half, hops) in enumerate(CHAINS):
            if half == h:
                drain(rb.at[n, hops - 1], r_ch.at[n, hops - 1])
                total = total + rb[n, hops - 1].astype(F32)
        ssum[h] = total
        remote(
            ssum.at[h, pl.ds(pl.multiple_of(32 * (1 - z), 32), 32), :],
            zr.at[h], s_z.at[h], r_z.at[h], (other_z, j),
        )
    half_rows = pl.ds(pl.multiple_of(32 * z, 32), 32)
    drain(zr.at[0], r_z.at[0])
    g = ssum[0, half_rows, :] + zr[0]
    act = g / (1.0 + jnp.exp(-g))
    drain(zr.at[1], r_z.at[1])
    hidden = (act * (ssum[1, half_rows, :] + zr[1])).astype(BF16)
    for t in range(2):
        hch[t] = hidden[16 * t : 16 * t + 16, :]
        for q in range(4):
            hpc[4 * t + q] = hidden[16 * t : 16 * t + 16, 128 * q : 128 * q + 128]

    def send_d1(q, _):
        unless_self(4 * q == j, hpc.at[q], hold.at[j], s_d1, r_d1, (i, 4 * q))
        return 0

    lax.fori_loop(0, 8, send_d1, 0)

    def send_row(q, _):
        k = 8 * c + q
        ic = i // 8
        dst = rowb.at[ic, q % 4, 2 * c + q // 4, i % 8]
        same = (j // 2 == i) & (2 * k + ic == j)
        unless_self(same, hpc.at[q], dst, s_row.at[0], r_row.at[0], (j // 2, 2 * k + ic))
        return 0

    lax.fori_loop(0, 8, send_row, 0)

    @pl.when(j % 4 == 0)
    def _():
        drain(hold, r_d1)
        obuf[0] = hold[panel[0]]
        obuf[1] = hold[pruned[0] // 4]
        obuf[2] = hold[pruned[1] // 4]

        def send_d2(d, _):
            remote(obuf, gbuf.at[j // 4], s_d2, r_d2, (i, (j + d) % NT))
            return 0

        lax.fori_loop(1, NT, send_d2, 0)
        here(obuf, gbuf.at[j // 4], r_d2)

    drain(gbuf, r_d2)
    for q in range(4):
        pcb[c, y, z, :, 128 * q : 128 * q + 128] = gbuf[4 * c + q, 0]
    for n in range(2):
        pcb[c, y, z, :, 512 + 128 * n : 640 + 128 * n] = gbuf[4 * c + pruned[n] % 4, 1 + n]
    order = (1, 7, 2, 6, 3, 5, 4)
    for d in order:
        remote(
            pcb.at[c, y, z], pcb.at[c, y, z], s_p.at[d], r_p.at[d], (2 * ((y + d) % NY) + z, j)
        )
    remote(pcb.at[c, y, z], pcb.at[c, y, z], s_pz, r_pz, (other_z, j))
    for d in order:
        got = pcb.at[c, (y + NY - d) % NY, z]
        drain(got, r_p.at[d])
        remote(got, got, s_pz, r_pz, (other_z, j))
    remote(pcb.at[c, :, z], pcb.at[c, :, z], s_ps, r_ps, (i, sib))
    drain(pcb.at[c, :, 1 - z], r_pz)
    remote(pcb.at[c, :, 1 - z], pcb.at[c, :, 1 - z], s_ps, r_ps, (i, sib))

    def send_col(d, _):
        remote(hch, colb.at[:, i], s_col, r_col, ((i + d) % NDP, j))
        return 0

    lax.fori_loop(1, NDP, send_col, 0)
    here(hch, colb.at[:, i], r_col)

    part0 = rowb.at[c, x, zh]
    drain(part0, r_row.at[0])
    for d in range(1, 4):
        remote(part0, part0, s_row.at[1], r_row.at[1], (i, (j + 8 * d) % NT))
    drain(rowb.at[c, x, pl.ds(0, 3)], r_row.at[1])
    part1 = rowb.at[c, x]
    for d in range(1, 4):
        remote(part1, part1, s_row.at[2], r_row.at[2], (i, zh * 8 + ((x + d) % 4) * 2 + c))
    drain(rowb.at[c, pl.ds(0, 3)], r_row.at[2])
    remote(rowb.at[c], rowb.at[c], s_row.at[3], r_row.at[3], (i, sib))

    drain(pcb.at[1 - c], r_ps)
    drain(colb, r_col)
    drain(pd, r_e2)
    drain(rowb.at[1 - c], r_row.at[3])
    drain(feat.at[c, pl.ds(0, 480)], s_tok)
    drain(feat.at[c], s_sib)
    for n, (way, h, hops) in enumerate(CHAINS):
        for s in range(hops):
            drain(sb.at[n, s], s_ch.at[n, s])
    for h in range(2):
        drain(zr.at[h], s_z.at[h])

    @pl.when(j % 4 == 0)
    def _():
        drain(hpc.at[pl.ds(0, 7)], s_d1)

        def wait_d2(d, _):
            drain(obuf, s_d2)
            return 0

        lax.fori_loop(1, NT, wait_d2, 0)

    @pl.when(j % 4 != 0)
    def _():
        drain(hpc, s_d1)

    self_row = (j // 2 == i) & ((j // 2) // 8 == c) & (i // 8 == c)

    @pl.when(self_row)
    def _():
        drain(hpc.at[pl.ds(0, 7)], s_row.at[0])

    @pl.when(jnp.logical_not(self_row))
    def _():
        drain(hpc, s_row.at[0])

    @pl.when(is_down_holder)
    def _():
        drain(dbuf.at[pl.ds(0, 15)], s_e1)

        def wait_e2(d, _):
            drain(dsel, s_e2)
            return 0

        lax.fori_loop(1, NT, wait_e2, 0)

    @pl.when(jnp.logical_not(is_down_holder))
    def _():
        drain(dbuf, s_e1)

    for d in order:
        drain(pcb.at[c, y, z], s_p.at[d])
    drain(pcb.at[c, :, z], s_pz)
    drain(pcb.at[c], s_ps)
    drain(colb.at[:, pl.ds(0, 15)], s_col)
    drain(rowb.at[c, x, pl.ds(0, 3)], s_row.at[1])
    drain(rowb.at[c, pl.ds(0, 3)], s_row.at[2])
    drain(rowb.at[c], s_row.at[3])


def spread(tokens, gate, up, down, pruned, panel):
    vmem = pl.BlockSpec(memory_space=pltpu.VMEM)
    smem = pl.BlockSpec(memory_space=pltpu.SMEM)
    dma = pltpu.SemaphoreType.DMA
    return pl.pallas_call(
        spread_kernel,
        out_shape=(
            jax.ShapeDtypeStruct((2, 4, 4, 8, 16, 128), BF16),
            jax.ShapeDtypeStruct((2, 16, 16, 512), BF16),
            jax.ShapeDtypeStruct((2, 8, 2, 16, 768), BF16),
            jax.ShapeDtypeStruct((16, 16, 512), BF16),
        ),
        in_specs=[vmem] * 4 + [smem] * 2,
        out_specs=(vmem,) * 4,
        scratch_shapes=[
            pltpu.VMEM((2, 512, 256), BF16),
            pltpu.VMEM((512, 1024), F32),
            pltpu.VMEM((4, 4, 64, 512), BF16),
            pltpu.VMEM((4, 4, 64, 512), BF16),
            pltpu.VMEM((2, 64, 512), F32),
            pltpu.VMEM((2, 32, 512), F32),
            pltpu.VMEM((2, 16, 512), BF16),
            pltpu.VMEM((8, 16, 128), BF16),
            pltpu.VMEM((32, 16, 128), BF16),
            pltpu.VMEM((3, 16, 128), BF16),
            pltpu.VMEM((8, 3, 16, 128), BF16),
            pltpu.VMEM((16, 16, 512), BF16),
            pltpu.VMEM((32, 16, 512), BF16),
            pltpu.VMEM((16, 512), BF16),
            dma, dma, dma, dma, dma((4, 4)), dma((4, 4)), dma((2,)), dma((2,)), dma, dma, dma, dma,
            dma((8,)), dma((8,)), dma, dma, dma, dma, dma((4,)), dma((4,)), dma, dma, dma, dma, dma, dma,
        ],
        compiler_params=pltpu.CompilerParams(
            collective_id=0, has_side_effects=True, vmem_limit_bytes=48 << 20
        ),
        name="spread",
    )(tokens, gate, up, down, pruned, panel)


def small_factor(p, w):
    low = [[None] * w for _ in range(w)]
    inv = [[None] * w for _ in range(w)]
    a = {(r, c): p[r][c] for r in range(w) for c in range(r + 1)}
    for c in range(w):
        s = lax.rsqrt(a[c, c])
        inv[c][c] = s
        for r in range(c + 1, w):
            low[r][c] = a[r, c] * s
        for r in range(c + 1, w):
            for q in range(c + 1, r + 1):
                a[r, q] = a[r, q] - low[r][c] * low[q][c]
    for r in range(w):
        for c in range(r):
            t = sum(low[r][k] * inv[k][c] for k in range(c, r))
            inv[r][c] = -(t * inv[r][r])
    return inv


def eliminate(t, w, n=128):
    lane = lax.broadcasted_iota(jnp.int32, (1, n), 1)
    m_rows, u_rows = [], []
    for k in range(0, n, w):
        base = n - t.shape[0]
        cols = [jnp.broadcast_to(t[:, k + q : k + q + 1], t.shape) for q in range(w)]
        p = [[cols[q][k + r - base : k + r - base + 1, :] for q in range(r + 1)] for r in range(w)]
        inv = small_factor(p, w)
        rows = [t[k + q - base : k + q - base + 1, :] for q in range(w)]
        inside = (lane >= k) & (lane < k + w)
        ident = [jnp.where(inside, (lane == k + q).astype(F32), rows[q]) for q in range(w)]
        for r in range(w):
            comb = sum(inv[r][q] * rows[q] for q in range(r + 1))
            m = jnp.where(lane < k, comb, 0.0)
            for q in range(r + 1):
                m = jnp.where(lane == k + q, inv[r][q], m)
            m_rows.append(m)
            u_rows.append(jnp.where(lane >= k + r, comb, 0.0))
        if k + w == n:
            break
        nb = ((k + w) // 8) * 8
        t = t[nb - base :, :]
        cols = [col[nb - base :, :] for col in cols]
        f = [sum(cols[q] * inv[r][q] for q in range(r + 1)) for r in range(w)]
        mult = [sum(f[r] * inv[r][q] for r in range(q, w)) for q in range(w)]
        t = jnp.where(inside, 0.0, t)
        for q in range(w):
            t = t - mult[q] * ident[q]
    return jnp.concatenate(m_rows, 0), jnp.concatenate(u_rows, 0)


def factor_panel(t_ref, m_ref, u_ref):
    zeros = jnp.zeros((128, 128), F32)
    for b in range(4):
        s0 = 128 * b
        m, u = eliminate(t_ref[s0 : s0 + 128, s0 : s0 + 128], WIDTH)
        s = dot3(m, t_ref[s0 : s0 + 128, :])
        parts = [s[:, 128 * q : 128 * q + 128] for q in range(4)]
        parts[b] = m
        for q in range(4):
            lanes = slice(128 * q, 128 * q + 128)
            m_ref[s0 : s0 + 128, lanes] = parts[q] if q <= b else zeros
            u_ref[s0 : s0 + 128, lanes] = parts[q] if q > b else (u if q == b else zeros)
        if b < 3:
            s = jnp.concatenate(parts, 1)
            rest = s0 + 128
            update = dot3(jnp.transpose(s[:, rest:]), s)
            for q in range(4):
                lanes = slice(128 * q, 128 * q + 128)
                old = t_ref[rest:, lanes] if q != b else 0.0
                t_ref[rest:, lanes] = old - update[:, lanes]


def finish_kernel(rowb, colb, pcb, pd, pruned, panel, fout, cout, t_ref, m_ref, u_ref):
    i = lax.axis_index("dp")
    j = lax.axis_index("tensor")
    p = panel[0]
    b0, b1 = pruned[0], pruned[1]
    lane = lax.broadcasted_iota(jnp.int32, (1, 512), 1)

    def kept(block512):
        blk = block512 * 4 + lane // 128
        return (blk != b0) & (blk != b1)

    def damping(keep):
        r = lax.broadcasted_iota(jnp.int32, (512, 512), 0)
        q = lax.broadcasted_iota(jnp.int32, (512, 512), 1)
        return jnp.where(r == q, jnp.where(keep, DAMPING, 1.0), 0.0)

    scale = 1.0 / 512
    p_kept = kept(p)
    c_kept = kept(j)
    hp = jnp.where(p_kept, pcb[:, :, :, :, :512].reshape(512, 512), 0.0).astype(BF16)
    hpr = pcb[:, :, :, :, 512:].reshape(512, 256)
    hc = jnp.where(c_kept, colb[...].reshape(512, 512), 0.0).astype(BF16)
    hpt = jnp.transpose(hp)
    hct = jnp.transpose(hc)
    t_ref[...] = dot(hpt, hp) * scale + damping(p_kept)
    kc = dot(hct, hp) * scale
    cross_c = (dot(hct, hpr) * scale).astype(BF16)
    cross_p = (dot(hpt, hpr) * scale).astype(BF16)

    factor_panel(t_ref, m_ref, u_ref)
    m = m_ref[...]
    below = (j > p).astype(F32)
    inside = (j == p).astype(F32)
    r = lax.broadcasted_iota(jnp.int32, (512, 512), 0)
    q = lax.broadcasted_iota(jnp.int32, (512, 512), 1)
    fc = dot3(kc, m, 1, 1) * below - jnp.where(r == q, inside, 0.0)
    gh, gl = split(dot3(fc, m))
    outside = 1.0 - inside
    rest = hc.astype(F32) * outside - (dot(hp, gh, 1, 1) + dot(hp, gl, 1, 1))
    zh, zl = split(cross_c.astype(F32) * outside - (dot(gh, cross_p) + dot(gl, cross_p)))
    down = pd[...].reshape(256, 512)
    cout[...] = dot(zh, down) + dot(zl, down)
    for h in range(2):
        row = 2 * i + h
        r_kept = kept(row)
        hr = jnp.concatenate(
            [
                jnp.concatenate(
                    [rowb[ic, cc, 2 * h + t].reshape(128, 128) for t in range(2) for ic in range(2)], 0
                )
                for cc in range(4)
            ],
            1,
        )
        hrt = jnp.transpose(jnp.where(r_kept, hr, 0.0).astype(BF16))
        rows = slice(512 * h, 512 * h + 512)

        @pl.when(row > p)
        def _():
            rh, rl = split(rest)
            fout[rows, :] = (dot(hrt, rh) + dot(hrt, rl)) * scale

        @pl.when(row <= p)
        def _():
            fout[rows, :] = dot(hrt, hc) * scale

        @pl.when(row == j)
        def _():
            fout[rows, :] += damping(r_kept)

        @pl.when((row == p) & (j == p))
        def _():
            fout[rows, :] = jnp.transpose(u_ref[...])


def finish(rowb, colb, pcb, pd, pruned, panel):
    vmem = pl.BlockSpec(memory_space=pltpu.VMEM)
    smem = pl.BlockSpec(memory_space=pltpu.SMEM)
    return pl.pallas_call(
        finish_kernel,
        out_shape=(jax.ShapeDtypeStruct((1024, 512), F32), jax.ShapeDtypeStruct((512, 512), F32)),
        in_specs=[vmem] * 4 + [smem] * 2,
        out_specs=(vmem,) * 2,
        scratch_shapes=[pltpu.VMEM((512, 512), F32)] * 3,
        compiler_params=pltpu.CompilerParams(vmem_limit_bytes=56 << 20),
        name="finish",
    )(rowb, colb, pcb, pd, pruned, panel)


def local(tokens, gate_weight, up_weight, down_weight, pruned_blocks, panel_number):
    spread_out = spread(tokens, gate_weight, up_weight, down_weight, pruned_blocks, panel_number)
    return finish(*spread_out, pruned_blocks, panel_number)


def solution(mesh):
    in_specs = (P("dp", None), P("dp", "tensor"), P("dp", "tensor"), P("tensor", "dp"), P(), P())
    out_specs = (P("dp", "tensor"), P("tensor", "dp"))
    return jax.shard_map(local, mesh=mesh, in_specs=in_specs, out_specs=out_specs, check_vma=False)
```

time: 726 us -> 132 us (0.18)
  the two profiles are of different devices: /device:TPU:16 before, /device:TPU:9 now
where the time goes in v1:
time: 132 us
  Pallas kernels  123 us (93%)
  local copies, waits for them, and re-layouts  8.19 us (6%)
    pallas_call x1, Pallas kernels, spread(): pl.pallas_call(spread_kernel, out_shape=(jax.ShapeDtypeStruct((2, 4, 4, 8...  93.4 us
    pallas_call x1, Pallas kernels, finish(): pl.pallas_call(finish_kernel, out_shape=(jax.ShapeDtypeStruct((1024, 512)...  29.1 us
    unnamed x18, local copies, waits for them, and re-layouts  8.19 us

profile of v1, /device:TPU:9, one launch (start us, length us, event | category | flops | bytes accessed | tf_op | source)
XLA Modules:
  0.0 132.0 jit_solution(5804275580546543640)
XLA Ops:
  1.3 0.0 copy-start.3
  1.3 1.0 copy-done.3
  2.3 0.0 copy-start.4
  2.3 1.0 copy-done.4
  3.4 0.0 copy-start.5
  3.4 1.0 copy-done.5
  4.4 0.0 copy-start.6
  4.4 1.0 copy-done.6
  5.4 0.0 copy-start.8
  5.4 0.7 copy-done.8
  6.1 93.4 %spread.1 = (bf16[2,4,4,8,16,128]{5,4,3,2,1,0:T(8,128)(2,1)S(1)}, bf16[2,16,16,512]{3,2,1,0:T(8,128)(2,1)S(1)}, bf16[2,8,2,16,768]{4,3,2,1,0:T(8,128)(2,1)S(1)}, bf16[16,16,512]{2,1,0:T(8,128)(2,1)S(1)}) custom-call(bf16[32,8192]{1,0:T(8,128)(2,1)S(1)} %copy-done.3, bf16[512,512]{1,0:T(8,128)(2,1)S(1)} %copy-done.4, bf16[512,512]{1,0:T(8,128)(2,1)S(1)} %copy-done.5, ...), custom_call_target="tpu_custom_call" | custom-call | tf_op jit(solution)/shard_map/spread/pallas_call | solution.py:307
  99.5 0.0 copy-start
  99.5 1.0 copy-done
  100.5 0.0 copy-start.1
  100.5 0.9 copy-done.1
  101.4 0.0 copy-start.2
  101.4 0.8 copy-done.2
  102.2 0.0 copy-start.7
  102.2 0.7 copy-done.7
  102.9 29.1 %finish.1 = (f32[1024,512]{1,0:T(8,128)}, f32[512,512]{1,0:T(8,128)}) custom-call(bf16[2,4,4,8,16,128]{5,4,3,2,1,0:T(8,128)(2,1)} %copy-done, bf16[2,16,16,512]{3,2,1,0:T(8,128)(2,1)} %copy-done.2, bf16[2,8,2,16,768]{4,3,2,1,0:T(8,128)(2,1)} %copy-done.1, bf16[16,16,512]{2,1,0:T(8,128)(2,1)} %copy-done.7, s32[2]{0:T(128)} %pruned.3, s32[1]{0:T(128)S(6)} %copy.8.panel), custom_call_target="tpu_custom_call" | custom-call | tf_op jit(solution)/shard_map/finish/pallas_call | solution.py:492
Async XLA Ops:
  1.3 1.0 copy-start.3
  2.3 1.0 copy-start.4
  3.4 1.0 copy-start.5
  4.4 1.0 copy-start.6
  5.4 0.7 copy-start.8
  99.5 1.0 copy-start
  100.5 0.9 copy-start.1
  101.4 0.8 copy-start.2
  102.2 0.7 copy-start.7

commit v2 on v0

v2 whole, which is shorter than its diff:
```python
import jax
import jax.numpy as jnp
from jax import lax
from jax.experimental import pallas as pl
from jax.experimental.pallas import tpu as pltpu
from jax.sharding import PartitionSpec as P

F32 = jnp.float32
BF16 = jnp.bfloat16
MESH = pl.DeviceIdType.MESH
DAMPING = 0.05
NDP = 16
NT = 32
NY = 8
WIDTH = 8

LONG = ((1, 0, 4), (-1, 2, 4), (1, 1, 4), (-1, 3, 4))
SHORT = ((1, 2, 3), (-1, 0, 3), (1, 3, 3), (-1, 1, 3))
CHAINS = LONG + SHORT


def split(x):
    hi = x.astype(BF16)
    return hi, (x - hi.astype(F32)).astype(BF16)


def dot(a, b, ca=1, cb=0):
    return lax.dot_general(a, b, (((ca,), (cb,)), ((), ())), preferred_element_type=F32)


def dot3(a, b, ca=1, cb=0):
    ah, al = split(a)
    bh, bl = split(b)
    return dot(ah, bh, ca, cb) + (dot(ah, bl, ca, cb) + dot(al, bh, ca, cb))


def eliminate(t, w, n=128):
    lane = lax.broadcasted_iota(jnp.int32, (1, n), 1)
    nb = w // 2
    m_rows, u_rows = [], []
    for k in range(0, n, w):
        base = n - t.shape[0]
        cols = [jnp.broadcast_to(t[:, k + q : k + q + 1], t.shape) for q in range(w)]
        a = {(r, q): cols[q][k + r - base : k + r - base + 1, :] for r in range(w) for q in range(r + 1)}
        rows = [t[k + q - base : k + q - base + 1, :] for q in range(w)]
        inside = (lane >= k) & (lane < k + w)
        ident = [jnp.where(inside, (lane == k + q).astype(F32), rows[q]) for q in range(w)]
        nxt = (k + w) // 8 * 8
        if k + w < n:
            cols = [col[nxt - base :, :] for col in cols]
            new = jnp.where(inside, 0.0, t[nxt - base :, :])
        for b in range(nb):
            i0, i1 = 2 * b, 2 * b + 1
            p, q, s = a[i0, i0], a[i1, i0], a[i1, i1]
            d = 1.0 / (p * s - q * q)
            ia, ib, ic = s * d, -(q * d), p * d
            r0 = lax.rsqrt(p)
            l = q * r0
            r1 = lax.rsqrt(s - l * l)
            for src, out, keep in ((ident, m_rows, lane < k + w), (rows, u_rows, None)):
                x0 = src[i0] * r0
                x1 = (src[i1] - x0 * l) * r1
                if keep is None:
                    out += [jnp.where(lane >= k + i0, x0, 0.0), jnp.where(lane >= k + i1, x1, 0.0)]
                else:
                    out += [jnp.where(keep, x0, 0.0), jnp.where(keep, x1, 0.0)]
            for r in range(i1 + 1, w):
                f0 = a[r, i0] * ia + a[r, i1] * ib
                f1 = a[r, i0] * ib + a[r, i1] * ic
                for c in range(i1 + 1, r + 1):
                    a[r, c] = a[r, c] - (f0 * a[c, i0] + f1 * a[c, i1])
                if k + w < n:
                    cols[r] = cols[r] - (cols[i0] * f0 + cols[i1] * f1)
                ident[r] = ident[r] - (f0 * ident[i0] + f1 * ident[i1])
                rows[r] = rows[r] - (f0 * rows[i0] + f1 * rows[i1])
            if k + w < n:
                g0 = ident[i0] * ia + ident[i1] * ib
                g1 = ident[i0] * ib + ident[i1] * ic
                new = new - (cols[i0] * g0 + cols[i1] * g1)
        if k + w < n:
            t = new
    return jnp.concatenate(m_rows, 0), jnp.concatenate(u_rows, 0)


def drain(ref, sem):
    pltpu.make_async_copy(ref, ref, sem).wait()


def body(
    tok_in, gate_in, up_in, down_in, pruned, panel,
    fout, cout,
    tok, gate, up, down, feat, pf, sb, rb, rl, zs_own, zr, hch, hpc, xb, zs, zr2, zb, zb2, pcb,
    colb, rowb, dx, dxr, dz, dzr, pd, t_ref, s_ref, m_ref, u_ref,
    s_in, hello, s_tok, r_tok, s_sib, r_sib, s_ch, r_ch, s_last, r_last, s_z, r_z,
    s_x, r_x, s_zh, r_zh, s_p, r_p, s_ps, r_ps, s_row, r_row, s_col, r_col, s_d, r_d,
):
    i = lax.axis_index("dp")
    j = lax.axis_index("tensor")
    y, z = i // 2, i % 2
    zh, x, c = j // 8, (j // 2) % 4, j % 2
    e8 = j % 8
    sib = j + 1 - 2 * c
    other_z = i + 1 - 2 * z

    def remote(src, dst, send, recv, to):
        pltpu.make_async_remote_copy(
            src_ref=src, dst_ref=dst, send_sem=send, recv_sem=recv, device_id=to, device_id_type=MESH
        ).start()

    def here(src, dst, sem):
        pltpu.make_async_copy(src, dst, sem).start()

    def signal(sem, to):
        pl.semaphore_signal(sem, inc=1, device_id=to, device_id_type=MESH)

    def line(d):
        return j - e8 + (e8 + d) % 8

    for n, (src, dst) in enumerate(((tok_in, tok), (gate_in, gate), (up_in, up), (down_in, down))):
        here(src, dst, s_in.at[n])

    barrier = pltpu.get_barrier_semaphore()

    def greet_dp(d, _):
        signal(barrier, ((i + d) % NDP, j))
        return 0

    def greet_line(d, _):
        signal(barrier, (i, line(d)))
        return 0

    def greet_zh(d, _):
        signal(barrier, (i, (j + 8 * d) % NT))
        return 0

    lax.fori_loop(1, NDP, greet_dp, 0)
    lax.fori_loop(1, 4, greet_zh, 0)
    lax.fori_loop(1, 8, greet_line, 0)
    drain(tok, s_in.at[0])
    pl.semaphore_wait(barrier, NDP - 1 + 3 + 7)

    def send_tok(o, g):
        src = tok.at[:, pl.ds(pl.multiple_of(512 * o + 256 * c, 256), 256)]
        dst = feat.at[c, y, pl.ds(pl.multiple_of(32 * z, 32), 32), :]
        remote(src, dst, s_tok, r_tok.at[g], (o, j))

    for g in (4, 3, 2, 1, 0):
        for way in (1, -1) if g in (1, 2, 3) else (1,):
            yo = (y + way * g + NY) % NY
            for zo in (z, 1 - z):
                if g == 0 and zo is z:
                    src = tok.at[:, pl.ds(pl.multiple_of(512 * i + 256 * c, 256), 256)]
                    here(src, feat.at[c, y, pl.ds(pl.multiple_of(32 * z, 32), 32), :], r_tok.at[0])
                else:
                    send_tok(2 * yo + zo, g)
    for d in range(1, 4):
        signal(hello, (i, (j + 8 * d) % NT))

    drain(down, s_in.at[3])
    for n in range(2):
        quarter = pruned[n] % 4
        for e in range(8):
            rows = [down[128 * k + 16 * e : 128 * k + 16 * e + 16, :] for k in range(4)]
            low = jnp.where(quarter == 0, rows[0], rows[1])
            high = jnp.where(quarter == 2, rows[2], rows[3])
            dx[e, n] = jnp.where(quarter < 2, low, high)

    def send_dx(d, _):
        e = (e8 + d) % 8
        remote(dx.at[e], dxr.at[e8], s_d.at[0], r_d.at[0], (i, line(d)))
        return 0

    lax.fori_loop(1, 8, send_dx, 0)
    here(dx.at[e8], dxr.at[e8], r_d.at[0])

    def blocks(g):
        return ((y + g) % NY, (y + NY - g) % NY) if g in (1, 2, 3) else ((y + g) % NY,)

    def forward(g):
        drain(feat.at[c, pl.ds(0, len(blocks(g)))], r_tok.at[g])
        for yb in blocks(g):
            remote(feat.at[c, yb], feat.at[c, yb], s_sib, r_sib.at[g], (i, sib))

    drain(gate, s_in.at[1])
    drain(up, s_in.at[2])

    def multiply(g):
        bs = blocks(g)
        drain(feat.at[c, pl.ds(0, len(bs))], r_sib.at[g])
        halves = [jnp.concatenate([feat[k, yb] for yb in bs], 0) for k in range(2)]
        for h, w in enumerate((gate, up)):
            v = dot(halves[0], w[:256, :]) + dot(halves[1], w[256:, :])
            for k, yb in enumerate(bs):
                pf[yb, :, 512 * h : 512 * h + 512] = v[64 * k : 64 * k + 64]

    def chain(n, s):
        way, h, hops = CHAINS[n]
        yd = (y + way * (hops - s + 1) + NY) % NY
        v = pf[yd, :, 256 * h : 256 * h + 256]
        if s > 1:
            drain(rb.at[n, s - 2], r_ch.at[n, s - 2])
            v = v + rb[n, s - 2].astype(F32)
        sb[n, s - 1] = v.astype(BF16)
        to = 2 * ((y + way + NY) % NY)
        if s < hops:
            remote(sb.at[n, s - 1], rb.at[n, s - 1], s_ch.at[n, s - 1], r_ch.at[n, s - 1], (to + z, j))
        else:
            for zo in (z, 1 - z):
                part = sb.at[n, s - 1, pl.ds(pl.multiple_of(32 * zo, 32), 32), :]
                remote(part, rl.at[n, z], s_last.at[n], r_last.at[n], (to + zo, j))

    def long(s):
        for n in range(4):
            chain(n, s)

    def short(s):
        for n in range(4, 8):
            chain(n, s)

    pl.semaphore_wait(hello, 3)
    forward(4)
    forward(3)
    multiply(4)
    long(1)
    forward(2)
    multiply(3)
    short(1)
    forward(1)
    multiply(2)
    long(2)
    drain(dxr, r_d.at[0])
    for n in range(2):
        dz[n] = dxr[(pruned[n] // 4) % 8, n]
    for d in range(1, 4):
        remote(dz, dzr.at[zh], s_d.at[1], r_d.at[1], (i, (j + 8 * d) % NT))
    here(dz, dzr.at[zh], r_d.at[1])
    short(2)
    forward(0)
    multiply(1)
    long(3)
    multiply(0)
    own_rows = pl.ds(pl.multiple_of(32 * z, 32), 32)
    zs_own[...] = pf[y, pl.ds(pl.multiple_of(32 * (1 - z), 32), 32), :].astype(BF16)
    remote(zs_own, zr, s_z, r_z, (other_z, j))
    short(3)
    long(4)
    drain(dzr, r_d.at[1])
    for n in range(2):
        pd[n, e8] = dzr[pruned[n] // 32, n]

    def send_pd(d, _):
        remote(pd.at[:, e8], pd.at[:, e8], s_d.at[2], r_d.at[2], (i, line(d)))
        return 0

    lax.fori_loop(1, 8, send_pd, 0)

    drain(zr, r_z)
    total = []
    for h in range(2):
        quarters = []
        for k in (2 * h, 2 * h + 1):
            v = pf[y, own_rows, 256 * k : 256 * k + 256] + zr[:, 256 * k : 256 * k + 256].astype(F32)
            for n in (4, 5, 6, 7, 0, 1, 2, 3):
                if CHAINS[n][1] == k:
                    drain(rl.at[n], r_last.at[n])
                    v = v + (rl[n, 0].astype(F32) + rl[n, 1].astype(F32))
            quarters.append(v)
        total.append(jnp.concatenate(quarters, 1))
    g, u = total
    hidden = (g / (1.0 + jnp.exp(-g)) * u).astype(BF16)
    for t in range(2):
        hch[t] = hidden[16 * t : 16 * t + 16, :]

    def send_x(d, _):
        e = (e8 + d) % 8
        remote(hch.at[e % 2], xb.at[e8], s_x, r_x, (i, line(d)))
        return 0

    lax.fori_loop(1, 8, send_x, 0)
    here(hch.at[c], xb.at[e8], r_x)

    for t in range(2):
        for q in range(4):
            hpc[4 * t + q] = hidden[16 * t : 16 * t + 16, 128 * q : 128 * q + 128]

    def send_row(q, _):
        k = 8 * c + q
        ic = i // 8
        dst = rowb.at[ic, q % 4, 2 * c + q // 4, i % 8]
        same = (j // 2 == i) & (2 * k + ic == j)

        @pl.when(same)
        def _():
            here(hpc.at[q], dst, r_row.at[0])

        @pl.when(jnp.logical_not(same))
        def _():
            remote(hpc.at[q], dst, s_row.at[0], r_row.at[0], (j // 2, 2 * k + ic))

        return 0

    lax.fori_loop(0, 8, send_row, 0)

    drain(xb, r_x)
    chosen = xb[panel[0] % 8]
    for q in range(4):
        zs[q] = chosen[:, 128 * q : 128 * q + 128]
    for d in range(1, 4):
        remote(zs, zb.at[zh], s_zh.at[0], r_zh.at[0], (i, (j + 8 * d) % NT))
    here(zs, zb.at[zh], r_zh.at[0])
    for n in range(2):
        quarter = pruned[n] % 4
        rows = [xb[(pruned[n] // 4) % 8, :, 128 * k : 128 * k + 128] for k in range(4)]
        low = jnp.where(quarter == 0, rows[0], rows[1])
        high = jnp.where(quarter == 2, rows[2], rows[3])
        zr2[n] = jnp.where(quarter < 2, low, high)
    for d in range(1, 4):
        remote(zr2, zb2.at[zh], s_zh.at[1], r_zh.at[1], (i, (j + 8 * d) % NT))
    here(zr2, zb2.at[zh], r_zh.at[1])

    def send_dp(part, n):
        def one(d, _):
            remote(part, part, s_p.at[n], r_p.at[n], ((i + d) % NDP, j))
            return 0

        lax.fori_loop(1, NDP, one, 0)

    def panel_part(n):
        return (pl.ds(0, 1), pl.ds(1, 3), pl.ds(4, 2))[n]

    drain(zb, r_zh.at[0])
    for q in range(4):
        pcb[c, i, q] = zb[panel[0] // 8, q]
    send_dp(pcb.at[c, i, panel_part(0)], 0)
    send_dp(pcb.at[c, i, panel_part(1)], 1)
    drain(zb2, r_zh.at[1])
    for n in range(2):
        pcb[c, i, 4 + n] = zb2[pruned[n] // 32, n]
    send_dp(pcb.at[c, i, panel_part(2)], 2)

    def send_col(d, _):
        remote(hch, colb.at[:, y, z], s_col.at[0], r_col.at[0], (2 * ((y + d) % NY) + z, j))
        return 0

    lax.fori_loop(1, NY, send_col, 0)
    here(hch, colb.at[:, y, z], r_col.at[0])

    def columns_over_z():
        same_z = colb.at[:, :, z]
        drain(same_z, r_col.at[0])
        remote(same_z, same_z, s_col.at[1], r_col.at[1], (other_z, j))

    def to_sibling(n):
        part = panel_part(n)
        drain(pcb.at[c, pl.ds(0, 15), part], r_p.at[n])
        remote(pcb.at[c, :, part], pcb.at[c, :, part], s_ps.at[n], r_ps.at[n], (i, sib))

    def from_sibling(n):
        drain(pcb.at[1 - c, :, panel_part(n)], r_ps.at[n])

    part0 = rowb.at[c, x, zh]
    part1 = rowb.at[c, x]
    part2 = rowb.at[c]

    def rows_over_z():
        drain(part0, r_row.at[0])
        for d in range(1, 4):
            remote(part0, part0, s_row.at[1], r_row.at[1], (i, (j + 8 * d) % NT))

    def rows_over_x():
        drain(rowb.at[c, x, pl.ds(0, 3)], r_row.at[1])
        for d in range(1, 4):
            remote(part1, part1, s_row.at[2], r_row.at[2], (i, zh * 8 + ((x + d) % 4) * 2 + c))

    def rows_over_cores():
        drain(rowb.at[c, pl.ds(0, 3)], r_row.at[2])
        remote(part2, part2, s_row.at[3], r_row.at[3], (i, sib))

    rows_over_z()
    to_sibling(0)

    lane = lax.broadcasted_iota(jnp.int32, (1, 512), 1)
    scale = 1.0 / 512
    b0, b1 = pruned[0], pruned[1]
    p = panel[0]

    def kept(block512):
        blk = block512 * 4 + lane // 128
        return (blk != b0) & (blk != b1)

    def damping(keep):
        n = keep.shape[1]
        r = lax.broadcasted_iota(jnp.int32, (n, n), 0)
        q = lax.broadcasted_iota(jnp.int32, (n, n), 1)
        return jnp.where(r == q, jnp.where(keep, DAMPING, 1.0), 0.0)

    p_kept = kept(p)
    from_sibling(0)
    hp0 = jnp.where(p_kept[:, :128], pcb[:, :, 0].reshape(512, 128), 0.0).astype(BF16)
    t_ref[:128, :128] = dot(jnp.transpose(hp0), hp0) * scale + damping(p_kept[:, :128])

    def factor_block(b, _):
        s0 = pl.multiple_of(128 * b, 128)
        at = pl.ds(s0, 128)
        m, u = eliminate(t_ref[at, at], WIDTH)

        @pl.when(b == 0)
        def _():
            to_sibling(1)
            from_sibling(1)
            hp = jnp.concatenate([pcb[:, :, q].reshape(512, 128) for q in range(4)], 1)
            hp = jnp.where(p_kept, hp, 0.0).astype(BF16)
            t_ref[...] = dot(jnp.transpose(hp), hp) * scale + damping(p_kept)
            to_sibling(2)
            rows_over_x()

        @pl.when(b == 1)
        def _():
            columns_over_z()

        @pl.when(b == 2)
        def _():
            rows_over_cores()

        lane_block = lane // 128
        s = dot3(m, t_ref[at, :])
        m_ref[at, :] = jnp.where(lane_block < b, s, 0.0)
        u_ref[at, :] = jnp.where(lane_block > b, s, 0.0)
        m_ref[at, at] = m
        u_ref[at, at] = u
        s_ref[...] = s
        s_ref[:, at] = m

        @pl.when(b < 3)
        def _():
            s = s_ref[...]
            update = dot3(jnp.transpose(s), s)
            row_block = lax.broadcasted_iota(jnp.int32, (512, 1), 0) // 128
            old = t_ref[...]
            t_ref[...] = jnp.where(row_block > b, jnp.where(lane_block == b, 0.0, old) - update, old)

        return 0

    lax.fori_loop(0, 4, factor_block, 0)

    from_sibling(2)
    hp = jnp.concatenate([pcb[:, :, q].reshape(512, 128) for q in range(4)], 1)
    hp = jnp.where(p_kept, hp, 0.0).astype(BF16)
    hpr = jnp.concatenate([pcb[:, :, 4 + q].reshape(512, 128) for q in range(2)], 1)
    hpt = jnp.transpose(hp)
    drain(colb.at[:, :, 1 - z], r_col.at[1])
    hc = jnp.where(kept(j), colb[...].reshape(512, 512), 0.0).astype(BF16)
    hct = jnp.transpose(hc)
    kc = dot(hct, hp) * scale
    cross_c = (dot(hct, hpr) * scale).astype(BF16)
    cross_p = (dot(hpt, hpr) * scale).astype(BF16)
    m = m_ref[...]
    below = (j > p).astype(F32)
    inside = (j == p).astype(F32)
    r = lax.broadcasted_iota(jnp.int32, (512, 512), 0)
    q = lax.broadcasted_iota(jnp.int32, (512, 512), 1)
    fc = dot3(kc, m, 1, 1) * below - jnp.where(r == q, inside, 0.0)
    gh, gl = split(dot3(fc, m))
    outside = 1.0 - inside
    rest = hc.astype(F32) * outside - (dot(hp, gh, 1, 1) + dot(hp, gl, 1, 1))
    rh, rlow = split(rest)
    ch, cl = split(cross_c.astype(F32) * outside - (dot(gh, cross_p) + dot(gl, cross_p)))
    drain(pd.at[:, pl.ds(0, 7)], r_d.at[2])
    chosen_down = pd[...].reshape(256, 512)
    cout[...] = dot(ch, chosen_down) + dot(cl, chosen_down)
    drain(rowb.at[1 - c], r_row.at[3])
    for h in range(2):
        row = 2 * i + h
        r_kept = kept(row)
        hr = jnp.concatenate(
            [
                jnp.concatenate(
                    [rowb[ic, cc, 2 * h + t].reshape(128, 128) for t in range(2) for ic in range(2)], 0
                )
                for cc in range(4)
            ],
            1,
        )
        hrt = jnp.transpose(jnp.where(r_kept, hr, 0.0).astype(BF16))
        under = row > p
        high = jnp.where(under, rh, hc)
        low = jnp.where(under, rlow, jnp.zeros_like(rlow))
        out = (dot(hrt, high) + dot(hrt, low)) * scale
        out = out + damping(r_kept) * (row == j).astype(F32)
        out = jnp.where((row == p) & (j == p), jnp.transpose(u_ref[...]), out)
        fout[512 * h : 512 * h + 512, :] = out

    drain(tok.at[:, pl.ds(0, 15 * 256)], s_tok)
    drain(feat.at[c], s_sib)
    for n, (way, h, hops) in enumerate(CHAINS):
        for s in range(hops - 1):
            drain(sb.at[n, s], s_ch.at[n, s])
        drain(rl.at[n], s_last.at[n])
    drain(zr, s_z)
    drain(xb.at[pl.ds(0, 7)], s_x)
    drain(zb.at[pl.ds(0, 3)], s_zh.at[0])
    drain(zb2.at[pl.ds(0, 3)], s_zh.at[1])
    for n in range(3):
        drain(pcb.at[c, pl.ds(0, 15), panel_part(n)], s_p.at[n])
        drain(pcb.at[c, :, panel_part(n)], s_ps.at[n])
    self_row = (j // 2 == i) & ((j // 2) // 8 == c) & (i // 8 == c)

    @pl.when(self_row)
    def _():
        drain(hpc.at[pl.ds(0, 7)], s_row.at[0])

    @pl.when(jnp.logical_not(self_row))
    def _():
        drain(hpc, s_row.at[0])

    drain(rowb.at[c, x, pl.ds(0, 3)], s_row.at[1])
    drain(rowb.at[c, pl.ds(0, 3)], s_row.at[2])
    drain(part2, s_row.at[3])
    drain(colb.at[:, pl.ds(0, 7), z], s_col.at[0])
    drain(colb.at[:, :, z], s_col.at[1])
    drain(dxr.at[pl.ds(0, 7)], s_d.at[0])
    drain(dzr.at[pl.ds(0, 3)], s_d.at[1])
    drain(pd.at[:, pl.ds(0, 7)], s_d.at[2])


def local(tokens, gate_weight, up_weight, down_weight, pruned_blocks, panel_number):
    vmem = pl.BlockSpec(memory_space=pltpu.VMEM)
    smem = pl.BlockSpec(memory_space=pltpu.SMEM)
    hbm = pl.BlockSpec(memory_space=pl.ANY)
    dma = pltpu.SemaphoreType.DMA

    def b16(*shape):
        return pltpu.VMEM(shape, BF16)

    def f32(*shape):
        return pltpu.VMEM(shape, F32)

    return pl.pallas_call(
        body,
        out_shape=(pltpu.VMEM((1024, 512), F32), pltpu.VMEM((512, 512), F32)),
        in_specs=[hbm] * 4 + [smem] * 2,
        out_specs=(vmem, vmem),
        scratch_shapes=[
            b16(32, 8192), b16(512, 512), b16(512, 512), b16(512, 512),
            b16(2, 8, 64, 256), f32(8, 64, 1024),
            b16(8, 4, 64, 256), b16(8, 3, 64, 256), b16(8, 2, 32, 256),
            b16(32, 1024), b16(32, 1024),
            b16(2, 16, 512), b16(8, 16, 128),
            b16(8, 16, 512),
            b16(4, 16, 128), b16(2, 16, 128), b16(4, 4, 16, 128), b16(4, 2, 16, 128),
            b16(2, 16, 6, 16, 128),
            b16(2, 8, 2, 16, 512), b16(2, 4, 4, 8, 16, 128),
            b16(8, 2, 16, 512), b16(8, 2, 16, 512), b16(2, 16, 512), b16(4, 2, 16, 512), b16(2, 8, 16, 512),
            f32(512, 512), f32(128, 512), f32(512, 512), f32(512, 512),
            dma((4,)), pltpu.SemaphoreType.REGULAR,
            dma, dma((5,)), dma, dma((5,)), dma((8, 3)), dma((8, 3)), dma((8,)), dma((8,)), dma, dma,
            dma, dma, dma((2,)), dma((2,)), dma((3,)), dma((3,)), dma((3,)), dma((3,)),
            dma((4,)), dma((4,)), dma((2,)), dma((2,)), dma((3,)), dma((3,)),
        ],
        compiler_params=pltpu.CompilerParams(
            collective_id=0, has_side_effects=True, vmem_limit_bytes=60 << 20
        ),
        name="prune",
    )(tokens, gate_weight, up_weight, down_weight, pruned_blocks, panel_number)


def solution(mesh):
    in_specs = (P("dp", None), P("dp", "tensor"), P("dp", "tensor"), P("tensor", "dp"), P(), P())
    out_specs = (P("dp", "tensor"), P("tensor", "dp"))
    return jax.shard_map(local, mesh=mesh, in_specs=in_specs, out_specs=out_specs, check_vma=False)
```

time: 726 us -> 85.2 us (0.12); the launches traced: 716 us -> 85.1 us
  waiting for transfers between devices: 443 us -> 0 us
  other arithmetic: 144 us -> 0 us
  Pallas kernels: 0 us -> 81.5 us
  matrix products: 45.6 us -> 0 us
  local copies, waits for them, and re-layouts: 38.5 us -> 2.29 us
  blocking collectives: 24.3 us -> 0 us
  between operations: 19.8 us -> 1.29 us
    psum x2 -> x0, waiting for transfers between devices: 443 us -> none  [the longest x1 296 us: spread_2(): return lax.psum(block, axis)]
    another operation x17 -> x0, other arithmetic: 133 us -> none  [the longest x14 91.7 us: local(): lower_factor = jnp.linalg.cholesky(diag_panel)]
    pallas_call x0 -> x1, Pallas kernels: none -> 81.5 us  [local(): pl.pallas_call(body, out_shape=(pltpu.VMEM((1024, 512), F32), pltpu.VMEM(...]
    all_to_all x1 -> x0, blocking collectives: 24.3 us -> none  [local(): lax.all_to_all(tokens, 'dp', split_axis=1, concat_axis=0, tiled=True)]
    another operation x27 -> x0, matrix products: 23.2 us -> none  [the longest x14 17.5 us: right_lower_solve(): lax.linalg.triangular_solve(lower_factor, columns, left_side=False, lower...]
    dot_general x9 -> x0, matrix products: 22.4 us -> none  [the longest x4 8.92 us: tokens_product(): lax.dot_general(left_side, right_side, (((0,), (0,)), ((), ())), preferre...]
    another operation x23 -> x0, local copies, waits for them, and re-layouts: 17.4 us -> none
    select_n x11 -> x0, other arithmetic: 7.88 us -> none  [the longest x4 5.31 us: spread_2(): jnp.where(lax.axis_index(axis) == owner, block, jnp.zeros_like(block))]
  transfers between devices with their start and end apart: 2 -> 0, of which waited for: 2 -> 0; matrix products, arithmetic and copies ran while one was open for 1% -> 0% of each run, Pallas kernels for 0% -> 0%
where the time goes in v2:
time: 85.2 us; the launch traced here: 85.1 us
  Pallas kernels  81.5 us (96%)
  local copies, waits for them, and re-layouts  2.29 us (3%)
  between operations  1.29 us (2%)
    pallas_call x1, Pallas kernels, local(): pl.pallas_call(body, out_shape=(pltpu.VMEM((1024, 512), F32), pltpu.VMEM(...  81.5 us
    unnamed x2, local copies, waits for them, and re-layouts  2.29 us

profile of v2, /device:TPU:16, one launch (start us, length us, event | category | flops | bytes accessed | tf_op | source)
XLA Modules:
  0.0 85.1 jit_solution(8318725085648625224)
XLA Ops:
  1.3 81.5 %prune.1 = (f32[1024,512]{1,0:T(8,128)S(1)}, f32[512,512]{1,0:T(8,128)S(1)}) custom-call(bf16[32,8192]{1,0:T(8,128)(2,1)} %tok_in.1, bf16[512,512]{1,0:T(8,128)(2,1)} %gate_in.1, bf16[512,512]{1,0:T(8,128)(2,1)} %up_in.1, bf16[512,512]{1,0:T(8,128)(2,1)} %down_in.1, s32[2]{0:T(128)} %pruned.1, s32[1]{0:T(128)S(6)} %copy.12.panel), custom_call_target="tpu_custom_call" | custom-call | tf_op jit(solution)/shard_map/prune/pallas_call | solution.py:538
  82.8 1.3 %copy.10 = f32[1024,512]{1,0:T(8,128)} copy(f32[1024,512]{1,0:T(8,128)S(1)} %get-tuple-element.2) | data formatting | bytes 4194304
  84.1 1.0 %copy.11 = f32[512,512]{1,0:T(8,128)} copy(f32[512,512]{1,0:T(8,128)S(1)} %get-tuple-element.3) | data formatting | bytes 2097152

commit v3 on v2

--- a/solution.py
+++ b/solution.py
@@ -29,8 +29,8 @@
 
 
 def dot3(a, b, ca=1, cb=0):
-    ah, al = split(a)
-    bh, bl = split(b)
+    ah, al = a if isinstance(a, tuple) else split(a)
+    bh, bl = b if isinstance(b, tuple) else split(b)
     return dot(ah, bh, ca, cb) + (dot(ah, bl, ca, cb) + dot(al, bh, ca, cb))
 
 
@@ -90,7 +90,7 @@
     tok_in, gate_in, up_in, down_in, pruned, panel,
     fout, cout,
     tok, gate, up, down, feat, pf, sb, rb, rl, zs_own, zr, hch, hpc, xb, zs, zr2, zb, zb2, pcb,
-    colb, rowb, dx, dxr, dz, dzr, pd, t_ref, s_ref, m_ref, u_ref,
+    colb, rowb, dx, dxr, dz, dzr, pd, t_ref, s_ref, m_ref, u_ref, hp_ref, hpt_ref,
     s_in, hello, s_tok, r_tok, s_sib, r_sib, s_ch, r_ch, s_last, r_last, s_z, r_z,
     s_x, r_x, s_zh, r_zh, s_p, r_p, s_ps, r_ps, s_row, r_row, s_col, r_col, s_d, r_d,
 ):
@@ -244,16 +244,6 @@
     remote(zs_own, zr, s_z, r_z, (other_z, j))
     short(3)
     long(4)
-    drain(dzr, r_d.at[1])
-    for n in range(2):
-        pd[n, e8] = dzr[pruned[n] // 32, n]
-
-    def send_pd(d, _):
-        remote(pd.at[:, e8], pd.at[:, e8], s_d.at[2], r_d.at[2], (i, line(d)))
-        return 0
-
-    lax.fori_loop(1, 8, send_pd, 0)
-
     drain(zr, r_z)
     total = []
     for h in range(2):
@@ -301,6 +291,16 @@
 
     lax.fori_loop(0, 8, send_row, 0)
 
+    drain(dzr, r_d.at[1])
+    for n in range(2):
+        pd[n, e8] = dzr[pruned[n] // 32, n]
+
+    def send_pd(d, _):
+        remote(pd.at[:, e8], pd.at[:, e8], s_d.at[2], r_d.at[2], (i, line(d)))
+        return 0
+
+    lax.fori_loop(1, 8, send_pd, 0)
+
     drain(xb, r_x)
     chosen = xb[panel[0] % 8]
     for q in range(4):
@@ -376,8 +376,8 @@
         drain(rowb.at[c, pl.ds(0, 3)], r_row.at[2])
         remote(part2, part2, s_row.at[3], r_row.at[3], (i, sib))
 
+    to_sibling(0)
     rows_over_z()
-    to_sibling(0)
 
     lane = lax.broadcasted_iota(jnp.int32, (1, 512), 1)
     scale = 1.0 / 512
@@ -410,7 +410,10 @@
             from_sibling(1)
             hp = jnp.concatenate([pcb[:, :, q].reshape(512, 128) for q in range(4)], 1)
             hp = jnp.where(p_kept, hp, 0.0).astype(BF16)
-            t_ref[...] = dot(jnp.transpose(hp), hp) * scale + damping(p_kept)
+            hp_ref[...] = hp
+            hpt = jnp.transpose(hp)
+            hpt_ref[...] = hpt
+            t_ref[...] = dot(hpt, hp) * scale + damping(p_kept)
             to_sibling(2)
             rows_over_x()
 
@@ -431,36 +434,44 @@
         s_ref[...] = s
         s_ref[:, at] = m
 
-        @pl.when(b < 3)
-        def _():
-            s = s_ref[...]
-            update = dot3(jnp.transpose(s), s)
-            row_block = lax.broadcasted_iota(jnp.int32, (512, 1), 0) // 128
-            old = t_ref[...]
-            t_ref[...] = jnp.where(row_block > b, jnp.where(lane_block == b, 0.0, old) - update, old)
+        for k in range(3):
+
+            @pl.when(b == k)
+            def _():
+                under = slice(128 * k + 128, 512)
+                parts = split(s_ref[...])
+                left = tuple(jnp.transpose(v[:, under]) for v in parts)
+                update = dot3(left, parts)
+                t_ref[under, under] -= update[:, under]
+                t_ref[under, : 128 * k + 128] = (
+                    jnp.where(lane[:, : 128 * k + 128] < 128 * k, t_ref[under, : 128 * k + 128], 0.0)
+                    - update[:, : 128 * k + 128]
+                )
 
         return 0
 
     lax.fori_loop(0, 4, factor_block, 0)
 
     from_sibling(2)
-    hp = jnp.concatenate([pcb[:, :, q].reshape(512, 128) for q in range(4)], 1)
-    hp = jnp.where(p_kept, hp, 0.0).astype(BF16)
+    hp = hp_ref[...]
     hpr = jnp.concatenate([pcb[:, :, 4 + q].reshape(512, 128) for q in range(2)], 1)
-    hpt = jnp.transpose(hp)
+    hpt = hpt_ref[...]
     drain(colb.at[:, :, 1 - z], r_col.at[1])
     hc = jnp.where(kept(j), colb[...].reshape(512, 512), 0.0).astype(BF16)
     hct = jnp.transpose(hc)
-    kc = dot(hct, hp) * scale
+    below = (j > p).astype(F32)
+    inside = (j == p).astype(F32)
+    kc = dot(hct, hp) * (scale * below)
     cross_c = (dot(hct, hpr) * scale).astype(BF16)
     cross_p = (dot(hpt, hpr) * scale).astype(BF16)
-    m = m_ref[...]
-    below = (j > p).astype(F32)
-    inside = (j == p).astype(F32)
-    r = lax.broadcasted_iota(jnp.int32, (512, 512), 0)
-    q = lax.broadcasted_iota(jnp.int32, (512, 512), 1)
-    fc = dot3(kc, m, 1, 1) * below - jnp.where(r == q, inside, 0.0)
-    gh, gl = split(dot3(fc, m))
+    m_parts = split(m_ref[...])
+    r = lax.broadcasted_iota(jnp.int32, (128, 128), 0)
+    q = lax.broadcasted_iota(jnp.int32, (128, 128), 1)
+    t_ref[...] = dot3(kc, m_parts, 1, 1)
+    for k in range(4):
+        at = slice(128 * k, 128 * k + 128)
+        t_ref[at, at] -= jnp.where(r == q, inside, 0.0)
+    gh, gl = split(dot3(t_ref[...], m_parts))
     outside = 1.0 - inside
     rest = hc.astype(F32) * outside - (dot(hp, gh, 1, 1) + dot(hp, gl, 1, 1))
     rh, rlow = split(rest)
@@ -469,6 +480,7 @@
     chosen_down = pd[...].reshape(256, 512)
     cout[...] = dot(ch, chosen_down) + dot(cl, chosen_down)
     drain(rowb.at[1 - c], r_row.at[3])
+    lower = jnp.transpose(u_ref[...])
     for h in range(2):
         row = 2 * i + h
         r_kept = kept(row)
@@ -486,9 +498,13 @@
         high = jnp.where(under, rh, hc)
         low = jnp.where(under, rlow, jnp.zeros_like(rlow))
         out = (dot(hrt, high) + dot(hrt, low)) * scale
-        out = out + damping(r_kept) * (row == j).astype(F32)
-        out = jnp.where((row == p) & (j == p), jnp.transpose(u_ref[...]), out)
-        fout[512 * h : 512 * h + 512, :] = out
+        rows = slice(512 * h, 512 * h + 512)
+        fout[rows, :] = jnp.where((row == p) & (j == p), lower, out)
+        on_diagonal = ((row == j) & (row != p)).astype(F32)
+        for k in range(4):
+            at = slice(128 * k, 128 * k + 128)
+            rows = slice(512 * h + 128 * k, 512 * h + 128 * k + 128)
+            fout[rows, at] += damping(r_kept[:, at]) * on_diagonal
 
     drain(tok.at[:, pl.ds(0, 15 * 256)], s_tok)
     drain(feat.at[c], s_sib)
@@ -552,6 +568,7 @@
             b16(2, 8, 2, 16, 512), b16(2, 4, 4, 8, 16, 128),
             b16(8, 2, 16, 512), b16(8, 2, 16, 512), b16(2, 16, 512), b16(4, 2, 16, 512), b16(2, 8, 16, 512),
             f32(512, 512), f32(128, 512), f32(512, 512), f32(512, 512),
+            b16(512, 512), b16(512, 512),
             dma((4,)), pltpu.SemaphoreType.REGULAR,
             dma, dma((5,)), dma, dma((5,)), dma((8, 3)), dma((8, 3)), dma((8,)), dma((8,)), dma, dma,
             dma, dma, dma((2,)), dma((2,)), dma((3,)), dma((3,)), dma((3,)), dma((3,)),

time: 85.2 us -> 84 us (0.986)
  Pallas kernels: 81.5 us -> 80.3 us
    pallas_call x1, Pallas kernels: 81.5 us -> 80.3 us  [local(): pl.pallas_call(body, out_shape=(pltpu.VMEM((1024, 512), F32), pltpu.VMEM(...]
where the time goes in v3:
time: 84 us; the launch traced here: 83.9 us
  Pallas kernels  80.3 us (96%)
  local copies, waits for them, and re-layouts  2.29 us (3%)
  between operations  1.29 us (2%)
    pallas_call x1, Pallas kernels, local(): pl.pallas_call(body, out_shape=(pltpu.VMEM((1024, 512), F32), pltpu.VMEM(...  80.3 us
    unnamed x2, local copies, waits for them, and re-layouts  2.29 us

profile of v3, /device:TPU:16, one launch (start us, length us, event | category | flops | bytes accessed | tf_op | source)
XLA Modules:
  0.0 83.9 jit_solution(15530875821923621957)
XLA Ops:
  1.3 80.3 %prune.1 = (f32[1024,512]{1,0:T(8,128)S(1)}, f32[512,512]{1,0:T(8,128)S(1)}) custom-call(bf16[32,8192]{1,0:T(8,128)(2,1)} %tok_in.1, bf16[512,512]{1,0:T(8,128)(2,1)} %gate_in.1, bf16[512,512]{1,0:T(8,128)(2,1)} %up_in.1, bf16[512,512]{1,0:T(8,128)(2,1)} %down_in.1, s32[2]{0:T(128)} %pruned.1, s32[1]{0:T(128)S(6)} %copy.12.panel), custom_call_target="tpu_custom_call" | custom-call | tf_op jit(solution)/shard_map/prune/pallas_call | solution.py:554
  81.6 1.3 %copy.10 = f32[1024,512]{1,0:T(8,128)} copy(f32[1024,512]{1,0:T(8,128)S(1)} %get-tuple-element.2) | data formatting | bytes 4194304
  82.9 1.0 %copy.11 = f32[512,512]{1,0:T(8,128)} copy(f32[512,512]{1,0:T(8,128)S(1)} %get-tuple-element.3) | data formatting | bytes 2097152

commit v4 on v3

--- a/solution.py
+++ b/solution.py
@@ -89,7 +89,7 @@
 def body(
     tok_in, gate_in, up_in, down_in, pruned, panel,
     fout, cout,
-    tok, gate, up, down, feat, pf, sb, rb, rl, zs_own, zr, hch, hpc, xb, zs, zr2, zb, zb2, pcb,
+    tok, gate, up, down, feat, pf, sb, sl, rb, rl, zs_own, zr, hch, hpc, xb, zs, zr2, zb, zb2, pcb,
     colb, rowb, dx, dxr, dz, dzr, pd, t_ref, s_ref, m_ref, u_ref, hp_ref, hpt_ref,
     s_in, hello, s_tok, r_tok, s_sib, r_sib, s_ch, r_ch, s_last, r_last, s_z, r_z,
     s_x, r_x, s_zh, r_zh, s_p, r_p, s_ps, r_ps, s_row, r_row, s_col, r_col, s_d, r_d,
@@ -200,13 +200,16 @@
         if s > 1:
             drain(rb.at[n, s - 2], r_ch.at[n, s - 2])
             v = v + rb[n, s - 2].astype(F32)
-        sb[n, s - 1] = v.astype(BF16)
+        if s < hops:
+            sb[n, s - 1] = v.astype(BF16)
+        else:
+            sl[n] = v
         to = 2 * ((y + way + NY) % NY)
         if s < hops:
             remote(sb.at[n, s - 1], rb.at[n, s - 1], s_ch.at[n, s - 1], r_ch.at[n, s - 1], (to + z, j))
         else:
             for zo in (z, 1 - z):
-                part = sb.at[n, s - 1, pl.ds(pl.multiple_of(32 * zo, 32), 32), :]
+                part = sl.at[n, pl.ds(pl.multiple_of(32 * zo, 32), 32), :]
                 remote(part, rl.at[n, z], s_last.at[n], r_last.at[n], (to + zo, j))
 
     def long(s):
@@ -253,7 +256,7 @@
             for n in (4, 5, 6, 7, 0, 1, 2, 3):
                 if CHAINS[n][1] == k:
                     drain(rl.at[n], r_last.at[n])
-                    v = v + (rl[n, 0].astype(F32) + rl[n, 1].astype(F32))
+                    v = v + (rl[n, 0] + rl[n, 1])
             quarters.append(v)
         total.append(jnp.concatenate(quarters, 1))
     g, u = total
@@ -559,7 +562,7 @@
         scratch_shapes=[
             b16(32, 8192), b16(512, 512), b16(512, 512), b16(512, 512),
             b16(2, 8, 64, 256), f32(8, 64, 1024),
-            b16(8, 4, 64, 256), b16(8, 3, 64, 256), b16(8, 2, 32, 256),
+            b16(8, 3, 64, 256), f32(8, 64, 256), b16(8, 3, 64, 256), f32(8, 2, 32, 256),
             b16(32, 1024), b16(32, 1024),
             b16(2, 16, 512), b16(8, 16, 128),
             b16(8, 16, 512),

time: 84 us -> 86.6 us (1.031)
  Pallas kernels: 80.3 us -> 82.8 us
    pallas_call x1, Pallas kernels: 80.3 us -> 82.8 us  [local(): pl.pallas_call(body, out_shape=(pltpu.VMEM((1024, 512), F32), pltpu.VMEM(...]
where the time goes in v4:
time: 86.6 us; the launch traced here: 86.4 us
  Pallas kernels  82.8 us (96%)
  local copies, waits for them, and re-layouts  2.29 us (3%)
  between operations  1.29 us (1%)
    pallas_call x1, Pallas kernels, local(): pl.pallas_call(body, out_shape=(pltpu.VMEM((1024, 512), F32), pltpu.VMEM(...  82.8 us
    unnamed x2, local copies, waits for them, and re-layouts  2.29 us

profile of v4, /device:TPU:16, one launch (start us, length us, event | category | flops | bytes accessed | tf_op | source)
XLA Modules:
  0.0 86.4 jit_solution(9582883473143522054)
XLA Ops:
  1.3 82.8 %prune.1 = (f32[1024,512]{1,0:T(8,128)S(1)}, f32[512,512]{1,0:T(8,128)S(1)}) custom-call(bf16[32,8192]{1,0:T(8,128)(2,1)} %tok_in.1, bf16[512,512]{1,0:T(8,128)(2,1)} %gate_in.1, bf16[512,512]{1,0:T(8,128)(2,1)} %up_in.1, bf16[512,512]{1,0:T(8,128)(2,1)} %down_in.1, s32[2]{0:T(128)} %pruned.1, s32[1]{0:T(128)S(6)} %copy.12.panel), custom_call_target="tpu_custom_call" | custom-call | tf_op jit(solution)/shard_map/prune/pallas_call | solution.py:557
  84.1 1.3 %copy.10 = f32[1024,512]{1,0:T(8,128)} copy(f32[1024,512]{1,0:T(8,128)S(1)} %get-tuple-element.2) | data formatting | bytes 4194304
  85.4 1.0 %copy.11 = f32[512,512]{1,0:T(8,128)} copy(f32[512,512]{1,0:T(8,128)S(1)} %get-tuple-element.3) | data formatting | bytes 2097152
